TPU v7x, 512 devices: a whole 4x8x8 slice. The times are simulated.
512 devices in a mesh: tm: 64 (over x, z, core), region: 8 (over y).
Axes of the slice: x: 4, y: 8, z: 8, core: 2. Of those that a mesh axis runs over, the one named last changes fastest.
Arguments:
- activity: bfloat16 [6144, 131072], P('region', 'tm'), may hold values from -6 to 6
- test_matrix: bfloat16 [131072, 512], P('tm', 'region'), may hold values from -0.015625 to 0.015625
- basis_mix: float32 [512, 64], replicated, may hold values from -0.25 to 0.25
- recurrent: float32 [64, 64], replicated, may hold values from -0.75 to 0.75
- latent_bias: float32 [64], replicated, may hold values from -2 to 2
- readout: bfloat16 [6144, 64], P('region'), may hold values from -0.75 to 0.75
- region_in: bfloat16 [6144, 8], P('region'), may hold values from -0.21875 to 0.21875
- region_out: bfloat16 [6144, 8], P('region'), may hold values from -1 to 1
- region_of_block: int32 [48], replicated, may hold values from 0 to 7, never falling along the last dimension, each value on 1 to 12 neighbouring positions
- region_mask: int32 [8, 8], replicated, may hold values 0 or 1
Outputs:
- latents: float32 [64, 131072], P(None, 'tm')
- frame_loss: float32 [131072], P('tm')
- readout_score: float32 [6144, 64], P('region')
Inputs may be any that keep to these rules, and one draw needn't show every extreme that they name: `region_of_block`: blocks of one region are consecutive, every region holds at least one block, and no region holds more than 12 blocks.
All inputs are finite; a program needn't handle non-finite values.
Results may differ from a plain program's by a relative error of at most 0.0028.
Values may be sent and summed in bfloat16 or wider, within the bound.
No kernel may reach another device: no remote copies, remote signals or barrier semaphores. Data moves between devices by JAX's collectives and lax.ppermute only.
A program may use at most 64 MiB of HBM per device.

v0:
```python
import jax
import jax.numpy as jnp
from jax import lax
from jax.sharding import PartitionSpec as P

BLOCK = 128
precise = lax.Precision.HIGHEST
epsilon = 1e-05


def from_behind(block, axis, distance):
    devices = range(lax.axis_size(axis))
    route = [(i - distance, i) for i in devices if i - distance in devices]
    return lax.ppermute(block, axis, route)


def orthonormal(sketch, gram):
    lower = jnp.linalg.cholesky(gram)
    return jax.scipy.linalg.solve_triangular(lower, sketch.T, lower=True).T


def region_tables(block_regions, region_mask, region_in, region_out):
    regions = region_mask.shape[0]
    signal_width = region_in.shape[1]
    block_total = block_regions.shape[0]
    block_rows = region_in.shape[0] // block_total
    onehot = (block_regions[:, None] == jnp.arange(regions, dtype=jnp.int32)[None, :]).astype(
        jnp.float32
    )
    onehot = jnp.broadcast_to(onehot[:, None, :], (block_total, block_rows, regions)).reshape(
        block_total * block_rows, regions
    )
    allowed = jnp.dot(onehot, region_mask.astype(jnp.float32), precision=precise)
    region_feed = (onehot[:, :, None] * region_in.astype(jnp.float32)[:, None, :]).reshape(
        -1, regions * signal_width
    )
    spread = (allowed[:, :, None] * region_out.astype(jnp.float32)[:, None, :]).reshape(
        -1, regions * signal_width
    )
    return (region_feed.astype(jnp.bfloat16), spread.astype(jnp.bfloat16))


def local(
    activity,
    test_matrix,
    basis_mix,
    recurrent,
    latent_bias,
    readout,
    region_in,
    region_out,
    region_of_block,
    region_mask,
):
    neurons_here, frames_here = activity.shape
    contract = (((0,), (0,)), ((), ()))
    block_count = neurons_here // BLOCK
    my_blocks = lax.dynamic_slice_in_dim(
        region_of_block, lax.axis_index("region") * block_count, block_count
    )
    region_feed, spread = region_tables(my_blocks, region_mask, region_in, region_out)
    test_full = lax.all_gather(test_matrix, "region", axis=1, tiled=True)
    sketch_rows = lax.psum_scatter(
        jnp.dot(activity, test_full, preferred_element_type=jnp.float32),
        "tm",
        scatter_dimension=0,
        tiled=True,
    )
    gram = lax.psum(jnp.dot(sketch_rows.T, sketch_rows, precision=precise), ("tm", "region"))
    loading_rows = jnp.dot(orthonormal(sketch_rows, gram), basis_mix, precision=precise).astype(
        jnp.bfloat16
    )
    latent_part = lax.dot_general(
        lax.all_gather(loading_rows, "tm", axis=0, tiled=True),
        activity,
        contract,
        preferred_element_type=jnp.float32,
    )
    signal_part = lax.dot_general(
        region_feed, activity, contract, preferred_element_type=jnp.float32
    )
    latents, signals = lax.psum((latent_part, signal_part), "region")
    prior_latent, prior_signal = from_behind((latents[:, -1:], signals[:, -1:]), "tm", 1)
    lagged_latents = jnp.concatenate([prior_latent, latents[:, :-1]], axis=1)
    lagged_signals = jnp.concatenate([prior_signal, signals[:, :-1]], axis=1)
    hidden = jnp.tanh(jnp.dot(recurrent, lagged_latents, precision=precise) + latent_bias[:, None])
    predicted = jnp.dot(readout, hidden.astype(jnp.bfloat16), preferred_element_type=jnp.float32)
    predicted = predicted + jnp.dot(
        spread, lagged_signals.astype(jnp.bfloat16), preferred_element_type=jnp.float32
    )
    error = activity.astype(jnp.float32) - predicted
    squared = error * error
    cross, error_sq, hidden_sq = lax.psum(
        (
            jnp.dot(error, hidden.T, precision=precise),
            jnp.sum(squared, axis=1),
            jnp.sum(hidden * hidden, axis=1),
        ),
        "tm",
    )
    frame_sq = lax.psum(jnp.sum(squared, axis=0), "region")
    frames_all = frames_here * lax.axis_size("tm")
    frame_loss = frame_sq / (neurons_here * lax.axis_size("region"))
    readout_score = cross / jnp.sqrt(
        frames_all
        * (error_sq[:, None] / frames_all + epsilon)
        * (hidden_sq[None, :] / frames_all + epsilon)
    )
    return (latents, frame_loss, readout_score)


def solution(mesh):
    in_specs = (
        P("region", "tm"),
        P("tm", "region"),
        P(),
        P(),
        P(),
        P("region", None),
        P("region", None),
        P("region", None),
        P(),
        P(),
    )
    out_specs = (P(None, "tm"), P("tm"), P("region", None))
    return jax.shard_map(local, mesh=mesh, in_specs=in_specs, out_specs=out_specs, check_vma=False)
```

profile of v0, /device:TPU:8, one launch (start us, length us, event | category | flops | bytes accessed | tf_op | source)
XLA Modules:
  0.0 1049.4 jit_solution(13345600834286897948)
XLA Ops:
  8.0 50.1 %all-gather.3.cloned.1.call-done = bf16[2048,512]{0,1:T(8,128)(2,1)} async-done(((bf16[2048,64]{0,1:T(8,128)(2,1)}), bf16[2048,512]{0,1:T(8,128)(2,1)}) %all-gather.3.cloned.1.call-update) | async-done | bytes 2097168 | tf_op jit(solution)/shard_map/all_gather | solution.py:62
  58.1 5.5 fusion.73
  63.6 141.2 %fusion = f32[16,512]{1,0:T(8,128)S(1)} fusion(f32[768,512]{1,0:T(8,128)} %fusion.73), kind=kCustom, calls=%all-reduce-scatter | all-reduce-scatter fusion | flops 524289 | bytes 1607680
  204.8 1.3 collective-permute-start.17
  206.1 1.3 collective-permute-start.16
  207.4 1.3 collective-permute-start.15
  208.7 1.3 collective-permute-start.14
  210.0 1.3 collective-permute-start.13
  211.3 1.3 collective-permute-start.12
  212.7 11.6 %collective-permute-start.11 = (f32[16,512]{1,0:T(8,128)S(1)}, f32[16,512]{1,0:T(8,128)S(1)}, u32[]{:S(2)}, u32[]{:S(2)}) collective-permute-start(f32[16,512]{1,0:T(8,128)S(1)} %fusion), channel_id=1, source_target_pairs={{0,80},{8,88},{16,96},{24,104},{32,112},{40,120},{48,128},{56,136}... | collective-permute-start | bytes 98312
  224.3 1.9 collective-permute-start.10
  226.3 5.7 collective-permute-start.9
  231.9 1.5 collective-permute-start.8
  233.4 3.8 collective-permute-start.7
  237.3 4.1 collective-permute-start.6
  241.5 3.3 collective-permute-start.5
  244.8 2.7 collective-permute-start.4
  247.5 2.5 collective-permute-start.3
  250.1 2.0 collective-permute-start.2
  252.9 1.3 dynamic-slice.7
  254.9 23.2 %concatenate.21 = f32[268,512]{1,0:T(8,128)} concatenate(f32[12,512]{1,0:T(8,128)S(1)} %collective-permute-done.17, f32[16,512]{1,0:T(8,128)S(1)} %collective-permute-done.16, f32[16,512]{1,0:T(8,128)S(1)} %collective-permute-done.15, f32[16,512]{1,0:T(8,128)S(1)} %collective-permute-done.14, f32[16,512]{1,0:T(8,128)S(1)} %collective-permute-done.13, ...), dimensions={0} | concatenate | bytes 1097728
  278.1 2.9 fusion.50
  281.6 1.5 fusion.26
  283.0 1.4 dynamic-slice_bitcast_fusion
  284.4 262.1 %all-reduce.9.cloned.1.call-done = f32[512,512]{0,1:T(8,128)} async-done(((f32[512,512]{0,1:T(8,128)}), f32[512,512]{0,1:T(8,128)}) %all-reduce.9.cloned.1.call-update) | async-done | bytes 1048592 | tf_op jit(solution)/shard_map/psum | solution.py:69
  546.5 2.6 copy.25
  549.1 1.8 fusion.4
  551.8 11.7 %cholesky.104 = f32[128,128]{1,0:T(8,128)S(1)} custom-call(f32[128,128]{1,0:T(8,128)S(1)} %cholesky.266), custom_call_target="Cholesky" | custom-call | tf_op jit(solution)/shard_map/jit(cholesky)/cholesky | solution.py:18
  563.6 9.8 custom-call.31
  573.4 1.1 cholesky.224
  574.5 1.9 constant_dynamic-update-slice_fusion.3
  576.5 1.3 convolution_subtract_fusion
  578.4 12.5 %cholesky.217 = f32[128,128]{1,0:T(8,128)S(1)} custom-call(f32[128,128]{1,0:T(8,128)} %cholesky.270), custom_call_target="Cholesky" | custom-call | tf_op jit(solution)/shard_map/jit(cholesky)/cholesky | solution.py:18
  591.6 10.8 %custom-call.32 = f32[1,128,128]{1,2,0:T(8,128)S(1)} custom-call(f32[1,128,128]{2,1,0:T(8,128)} %get-tuple-element.31), custom_call_target="InvertDiagBlocksLowerTriangular" | custom-call | tf_op jit(solution)/shard_map/jit(cholesky)/cholesky | solution.py:18
  603.3 1.4 convolution_subtract_fusion.1
  604.8 11.7 %cholesky.238 = f32[128,128]{1,0:T(8,128)S(1)} custom-call(f32[128,128]{1,0:T(8,128)S(1)} %cholesky.275), custom_call_target="Cholesky" | custom-call | tf_op jit(solution)/shard_map/jit(cholesky)/cholesky | solution.py:18
  617.8 9.8 custom-call.33
  628.4 1.4 convolution_subtract_fusion.2
  629.9 11.9 %cholesky.255 = f32[128,128]{1,0:T(8,128)S(1)} custom-call(f32[128,128]{1,0:T(8,128)S(1)} %convolution_subtract_fusion.2), custom_call_target="Cholesky" | custom-call | tf_op jit(solution)/shard_map/jit(cholesky)/cholesky | solution.py:18
  646.3 2.3 select_select_fusion
  648.6 14.4 %while.1 = (s32[]{:T(128)}, f32[512,512]{1,0:T(8,128)}, s32[4,2]{0,1:T(2,128)S(1)}, f32[4,128,128]{2,1,0:T(8,128)}, s32[]{:T(128)}) while((s32[]{:T(128)}, f32[512,512]{1,0:T(8,128)}, s32[4,2]{0,1:T(2,128)S(1)}, f32[4,128,128]{2,1,0:T(8,128)}, s32[]{:T(128)}) %tuple.34), condition=%wide.while_cond, body=%wide.while_body.sunk | while | flops 2 | bytes 132205 | solution.py:19
  649.3 3.0 bitcast_dynamic-update-slice_fusion.2
  652.9 3.0 bitcast_dynamic-update-slice_fusion.2
  656.5 3.0 bitcast_dynamic-update-slice_fusion.2
  660.1 2.9 bitcast_dynamic-update-slice_fusion.2
  663.0 40.1 %custom-call.34 = f32[4,128,128]{1,2,0:T(8,128)S(1)} custom-call(f32[4,128,128]{2,1,0:T(8,128)} %get-tuple-element.10), custom_call_target="InvertDiagBlocksLowerTriangular" | custom-call | tf_op jit(solution)/shard_map/jit(_solve_triangular)/triangular_solve | solution.py:19
  705.9 1.1 fusion.19
  707.9 1.3 fusion.14
  710.3 43.1 %all-gather = bf16[64,12,64]{2,1,0:T(8,128)(2,1)S(1)} all-gather(bf16[1,12,64]{2,1,0:T(8,128)(2,1)S(1)} %fusion.3), channel_id=1, replica_groups=mesh['tm'=64,'region'=8] {'tm'}, dimensions={0}, use_global_device_ids=true | all-gather | bytes 99840 | tf_op jit(solution)/shard_map/all_gather | solution.py:74
  754.2 2.4 fusion.74
  756.7 35.5 %all-reduce.14 = bf16[64,2048]{1,0:T(8,128)(2,1)S(1)} all-reduce(f32[64,2048]{1,0:T(8,128)} %fusion.26), channel_id=1, replica_groups=mesh['tm'=64,'region'=8] {'region'}, use_global_device_ids=true, to_apply=%region_11.12 | all-reduce | flops 131072 | bytes 786432 | tf_op jit(solution)/shard_map/psum | solution.py:82
  792.8 1.9 collective-permute-start.1
  794.7 36.6 %all-reduce.11.cloned.1.call-done = f32[64,2048]{1,0:T(8,128)} async-done(((f32[64,2048]{1,0:T(8,128)}), f32[64,2048]{1,0:T(8,128)}) %all-reduce.11.cloned.1.call-update) | async-done | bytes 524304 | tf_op jit(solution)/shard_map/psum | solution.py:82
  831.3 1.4 slice.142
  832.7 2.1 collective-permute-start
  835.7 2.8 copy.26
  838.6 1.9 multiply_reduce_fusion.2
  840.5 2.1 fusion.12
  842.6 2.5 multiply_reduce_fusion
  845.2 4.8 fusion.75
  850.0 129.4 %all-reduce.3 = (f32[64]{0:T(128)S(1)}, f32[768]{0:T(1024)S(1)}) all-reduce(f32[64]{0:T(128)S(1)} %get-tuple-element.38, f32[768]{0:T(1024)S(1)} %get-tuple-element.11), channel_id=1, replica_groups=mesh['tm'=64,'region'=8] {'tm'}, use_global_device_ids=true, to_apply=%region_18.19 | all-reduce | flops 832 | bytes 6656 | tf_op jit(solution)/shard_map/psum | solution.py:93
  979.4 15.0 %psum.52 = f32[2048]{0:T(1024)S(1)} all-reduce(f32[2048]{0:T(1024)S(1)} %get-tuple-element.12), channel_id=1, replica_groups=mesh['tm'=64,'region'=8] {'region'}, use_global_device_ids=true, to_apply=%region_13.14 | all-reduce | flops 2048 | bytes 16384 | tf_op jit(solution)/shard_map/psum | solution.py:101
  995.0 45.1 %all-reduce.13.cloned.1.call-done = f32[768,64]{0,1:T(8,128)} async-done(((f32[768,64]{0,1:T(8,128)}), f32[768,64]{0,1:T(8,128)}) %all-reduce.13.cloned.1.call-update) | async-done | bytes 196624 | tf_op jit(solution)/shard_map/psum | solution.py:93
  1040.1 1.7 rsqrt_multiply_fusion
  (102 shorter events, 20.9 us)
Async XLA Ops:
  7.2 702.9 %copy-start = (f32[512,64]{0,1:T(8,128)S(1)}, f32[512,64]{0,1:T(8,128)}, u32[]{:S(2)}) copy-start(f32[512,64]{0,1:T(8,128)} %param.12) | copy-start | bytes 393220
  7.2 50.9 %all-gather.3.cloned.1.call-start = ((), (), s32[]{:S(2)}) async-start(), calls=%async_computation | async-start | bytes 2359296 | tf_op jit(solution)/shard_map/all_gather | solution.py:62
  7.9 204.7 %copy-start.16 = (s32[48]{0:T(128)S(1)}, s32[48]{0:T(128)}, u32[]{:S(2)}) copy-start(s32[48]{0:T(128)} %param.18) | copy-start | bytes 580
  7.9 538.6 %all-reduce.9.cloned.1.call-start = ((), (), s32[]{:S(2)}) async-start(), calls=%async_computation.1 | async-start | bytes 2097152 | tf_op jit(solution)/shard_map/psum | solution.py:69
  63.6 218.0 %copy-start.1 = (bf16[768,2048]{1,0:T(8,128)(2,1)S(1)}, bf16[768,2048]{1,0:T(8,128)(2,1)}, u32[]{:S(2)}) copy-start(bf16[768,2048]{1,0:T(8,128)(2,1)} %param.10) | copy-start | bytes 9437188
  204.8 6.5 collective-permute-start.17
  206.1 6.6 collective-permute-start.16
  207.4 16.9 %collective-permute-start.15 = (f32[16,512]{1,0:T(8,128)S(1)}, f32[16,512]{1,0:T(8,128)S(1)}, u32[]{:S(2)}, u32[]{:S(2)}) collective-permute-start(f32[16,512]{1,0:T(8,128)S(1)} %fusion), channel_id=1, source_target_pairs={{0,112},{8,120},{16,128},{24,136},{32,144},{40,152},{48,160},{56,1... | collective-permute-start | bytes 98312
  208.7 17.5 %collective-permute-start.14 = (f32[16,512]{1,0:T(8,128)S(1)}, f32[16,512]{1,0:T(8,128)S(1)}, u32[]{:S(2)}, u32[]{:S(2)}) collective-permute-start(f32[16,512]{1,0:T(8,128)S(1)} %fusion), channel_id=1, source_target_pairs={{0,104},{8,112},{16,120},{24,128},{32,136},{40,144},{48,152},{56,1... | collective-permute-start | bytes 98312
  210.0 21.9 %collective-permute-start.13 = (f32[16,512]{1,0:T(8,128)S(1)}, f32[16,512]{1,0:T(8,128)S(1)}, u32[]{:S(2)}, u32[]{:S(2)}) collective-permute-start(f32[16,512]{1,0:T(8,128)S(1)} %fusion), channel_id=1, source_target_pairs={{0,96},{8,104},{16,112},{24,120},{32,128},{40,136},{48,144},{56,15... | collective-permute-start | bytes 98312
  211.3 22.1 %collective-permute-start.12 = (f32[16,512]{1,0:T(8,128)S(1)}, f32[16,512]{1,0:T(8,128)S(1)}, u32[]{:S(2)}, u32[]{:S(2)}) collective-permute-start(f32[16,512]{1,0:T(8,128)S(1)} %fusion), channel_id=1, source_target_pairs={{0,88},{8,96},{16,104},{24,112},{32,120},{40,128},{48,136},{56,144... | collective-permute-start | bytes 98312
  212.7 24.6 %collective-permute-start.11 = (f32[16,512]{1,0:T(8,128)S(1)}, f32[16,512]{1,0:T(8,128)S(1)}, u32[]{:S(2)}, u32[]{:S(2)}) collective-permute-start(f32[16,512]{1,0:T(8,128)S(1)} %fusion), channel_id=1, source_target_pairs={{0,80},{8,88},{16,96},{24,104},{32,112},{40,120},{48,128},{56,136}... | collective-permute-start | bytes 98312
  224.3 17.2 %collective-permute-start.10 = (f32[16,512]{1,0:T(8,128)S(1)}, f32[16,512]{1,0:T(8,128)S(1)}, u32[]{:S(2)}, u32[]{:S(2)}) collective-permute-start(f32[16,512]{1,0:T(8,128)S(1)} %fusion), channel_id=1, source_target_pairs={{0,72},{8,80},{16,88},{24,96},{32,104},{40,112},{48,120},{56,128},... | collective-permute-start | bytes 98312
  226.3 18.6 %collective-permute-start.9 = (f32[16,512]{1,0:T(8,128)S(1)}, f32[16,512]{1,0:T(8,128)S(1)}, u32[]{:S(2)}, u32[]{:S(2)}) collective-permute-start(f32[16,512]{1,0:T(8,128)S(1)} %fusion), channel_id=1, source_target_pairs={{0,64},{8,72},{16,80},{24,88},{32,96},{40,104},{48,112},{56,120},{... | collective-permute-start | bytes 98312
  231.9 15.6 %collective-permute-start.8 = (f32[16,512]{1,0:T(8,128)S(1)}, f32[16,512]{1,0:T(8,128)S(1)}, u32[]{:S(2)}, u32[]{:S(2)}) collective-permute-start(f32[16,512]{1,0:T(8,128)S(1)} %fusion), channel_id=1, source_target_pairs={{0,56},{8,64},{16,72},{24,80},{32,88},{40,96},{48,104},{56,112},{6... | collective-permute-start | bytes 98312
  233.4 16.7 %collective-permute-start.7 = (f32[16,512]{1,0:T(8,128)S(1)}, f32[16,512]{1,0:T(8,128)S(1)}, u32[]{:S(2)}, u32[]{:S(2)}) collective-permute-start(f32[16,512]{1,0:T(8,128)S(1)} %fusion), channel_id=1, source_target_pairs={{0,48},{8,56},{16,64},{24,72},{32,80},{40,88},{48,96},{56,104},{64... | collective-permute-start | bytes 98312
  237.3 14.9 %copy-start.11 = (f32[6,8]{1,0:T(8,128)}, f32[6,8]{1,0:T(8,128)S(1)}, u32[]{:S(2)}) copy-start(f32[6,8]{1,0:T(8,128)S(1)} %fusion.66) | copy-start | bytes 580
  237.3 12.7 %copy-start.5 = (f32[16,512]{1,0:T(8,128)}, f32[16,512]{1,0:T(8,128)S(1)}, u32[]{:S(2)}) copy-start(f32[16,512]{1,0:T(8,128)S(1)} %collective-permute-done.11) | copy-start | bytes 98308
  237.3 17.5 %collective-permute-start.6 = (f32[16,512]{1,0:T(8,128)S(1)}, f32[16,512]{1,0:T(8,128)}, u32[]{:S(2)}, u32[]{:S(2)}) collective-permute-start(f32[16,512]{1,0:T(8,128)S(1)} %fusion), channel_id=1, source_target_pairs={{0,40},{8,48},{16,56},{24,64},{32,72},{40,80},{48,88},{56,96},{64,... | collective-permute-start | bytes 98312
  241.5 10.6 %copy-start.6 = (f32[16,512]{1,0:T(8,128)}, f32[16,512]{1,0:T(8,128)S(1)}, u32[]{:S(2)}) copy-start(f32[16,512]{1,0:T(8,128)S(1)} %collective-permute-done.10) | copy-start | bytes 98308
  241.5 13.4 %collective-permute-start.5 = (f32[16,512]{1,0:T(8,128)S(1)}, f32[16,512]{1,0:T(8,128)}, u32[]{:S(2)}, u32[]{:S(2)}) collective-permute-start(f32[16,512]{1,0:T(8,128)S(1)} %fusion), channel_id=1, source_target_pairs={{0,32},{8,40},{16,48},{24,56},{32,64},{40,72},{48,80},{56,88},{64,... | collective-permute-start | bytes 98312
  244.8 7.4 copy-start.7
  244.8 10.1 collective-permute-start.4
  247.5 4.7 copy-start.8
  247.5 7.4 collective-permute-start.3
  250.1 2.1 copy-start.9
  250.1 4.8 collective-permute-start.2
  281.0 550.3 %all-reduce.11.cloned.1.call-start = ((), (), s32[]{:S(2)}) async-start(), calls=%async_computation.2 | async-start | bytes 1048576 | tf_op jit(solution)/shard_map/psum | solution.py:82
  550.9 1.0 copy-start.3
  709.2 125.7 %copy-start.12 = (f32[6,8]{1,0:T(8,128)S(1)}, f32[6,8]{1,0:T(8,128)}, u32[]{:S(2)}) copy-start(f32[6,8]{1,0:T(8,128)} %copy-done.11) | copy-start | bytes 580
  709.2 125.7 %copy-start.15 = (s32[8,8]{1,0:T(8,128)S(1)}, s32[8,8]{1,0:T(8,128)}, u32[]{:S(2)}) copy-start(s32[8,8]{1,0:T(8,128)} %param.19) | copy-start | bytes 772
  756.6 283.5 %all-reduce.13.cloned.1.call-start = ((), (), s32[]{:S(2)}) async-start(), calls=%async_computation.3 | async-start | bytes 393216 | tf_op jit(solution)/shard_map/psum | solution.py:93
  792.8 49.8 %collective-permute-start.1 = (bf16[64,1]{1,0:T(8,128)(2,1)}, bf16[64,1]{1,0:T(8,128)(2,1)}, u32[]{:S(2)}, u32[]{:S(2)}) collective-permute-start(bf16[64,1]{1,0:T(8,128)(2,1)} %slice.144), channel_id=1, source_target_pairs={{0,8},{8,16},{16,24},{24,32},{32,40},{40,48},{48,56},{56,64},{64,7... | collective-permute-start | bytes 392 | tf_op jit(solution)/shard_map/ppermute | solution.py:14
  832.7 5.8 collective-permute-start
  835.7 2.8 copy-start.13
  835.7 2.8 copy-start.14
  840.5 2.1 copy-start.2
  840.5 2.1 copy-start.10
  845.1 196.6 %copy-start.4 = (f32[64,2048]{1,0:T(8,128)S(1)}, f32[64,2048]{1,0:T(8,128)}, u32[]{:S(2)}) copy-start(f32[64,2048]{1,0:T(8,128)} %all-reduce.11.cloned.1.call-done) | copy-start | bytes 1572868
Sparse Core Ops, SparseCore 0:
  10.1 47.9 all-gather.2
  281.1 265.3 all-reduce.8
  756.7 74.5 all-reduce.10
  850.1 189.9 all-reduce.12
where the time goes:
time: 1060 us; the launch traced here: 1050 us
  waiting for transfers between devices  395 us (37%)
  blocking collectives  364 us (34%)
  other arithmetic  130 us (12%)
  local copies, waits for them, and re-layouts  52.3 us (5%)
  starting transfers between devices  51.6 us (5%)
  matrix products  39.4 us (4%)
  between operations  17.7 us (2%)
    psum x1, waiting for transfers between devices, local(): lax.psum(jnp.dot(sketch_rows.T, sketch_rows, precision=precise), ('tm', '...  262 us
    unnamed x1, blocking collectives  141 us
    psum x1, blocking collectives, local(): lax.psum((jnp.dot(error, hidden.T, precision=precise), jnp.sum(squared, a...  129 us
    another operation x14, other arithmetic, orthonormal(): lower = jnp.linalg.cholesky(gram)  82.2 us
    all_gather x1, waiting for transfers between devices, local(): test_full = lax.all_gather(test_matrix, 'region', axis=1, tiled=True)  50.1 us
    unnamed x16, starting transfers between devices  47 us
    psum x1, waiting for transfers between devices, local(): lax.psum((jnp.dot(error, hidden.T, precision=precise), jnp.sum(squared, a...  45.1 us
    all_gather x1, blocking collectives, local(): lax.all_gather(loading_rows, 'tm', axis=0, tiled=True)  43.1 us
  transfers between devices with their start and end apart: 22, of which 4 were waited for; matrix products, arithmetic and copies ran while one was open for 1% of the time, Pallas kernels for 0%

commit v1 on v0

--- a/solution.py
+++ b/solution.py
@@ -1,3 +1,4 @@
+import functools
 import jax
 import jax.numpy as jnp
 from jax import lax
@@ -6,6 +7,24 @@
 BLOCK = 128
 precise = lax.Precision.HIGHEST
 epsilon = 1e-05
+
+
+def carry_outputs(incoming_x, axis_tag):
+    state_now, tmp, upper = (lax.axis_size(axis_tag), lax.axis_index(axis_tag), incoming_x.shape[1])
+    table = [(h, (h + 1) % state_now) for h in range(state_now)]
+    extra = jnp.zeros(
+        (*incoming_x.shape[:1], state_now * upper, *incoming_x.shape[2:]), incoming_x.dtype
+    )
+    ready = incoming_x
+    for idx in range(state_now):
+        last = (tmp - idx) % state_now
+        extra = lax.dynamic_update_slice_in_dim(extra, ready, last * upper, axis=1)
+        if idx < state_now - 1:
+            ready = lax.ppermute(ready, axis_name=axis_tag, perm=table)
+    return extra
+
+
+shelves_store = functools.partial(carry_outputs, axis_tag="region")
 
 
 def from_behind(block, axis, distance):
@@ -59,7 +78,7 @@
         region_of_block, lax.axis_index("region") * block_count, block_count
     )
     region_feed, spread = region_tables(my_blocks, region_mask, region_in, region_out)
-    test_full = lax.all_gather(test_matrix, "region", axis=1, tiled=True)
+    test_full = shelves_store(test_matrix)
     sketch_rows = lax.psum_scatter(
         jnp.dot(activity, test_full, preferred_element_type=jnp.float32),
         "tm",

time: 1060 us -> 1070 us (level)
  waiting for transfers between devices: 395 us -> 605 us
  blocking collectives: 364 us -> 223 us
  starting transfers between devices: 51.6 us -> 19.7 us
  local copies, waits for them, and re-layouts: 52.3 us -> 34.1 us
    unnamed x20 -> x5, waiting for transfers between devices: 0.77 us -> 196 us
    unnamed x1 -> x0, blocking collectives: 141 us -> none
    ppermute x0 -> x7, waiting for transfers between devices: none -> 59.3 us  [carry_outputs(): ready = lax.ppermute(ready, axis_name=axis_tag, perm=table)]
    all_gather x1 -> x0, waiting for transfers between devices: 50.1 us -> none  [local(): test_full = lax.all_gather(test_matrix, 'region', axis=1, tiled=True)]
    unnamed x16 -> x1, starting transfers between devices: 47 us -> 0.04 us
    unnamed x40 -> x37, local copies, waits for them, and re-layouts: 29.9 us -> 9.26 us
    ppermute x0 -> x7, starting transfers between devices: none -> 15.1 us  [carry_outputs(): ready = lax.ppermute(ready, axis_name=axis_tag, perm=table)]
  transfers between devices with their start and end apart: 22 -> 13, of which waited for: 4 -> 11; matrix products, arithmetic and copies ran while one was open for 1% -> 2% of each run, Pallas kernels for 0% -> 0%
where the time goes in v1:
time: 1070 us; the launch traced here: 1060 us
  waiting for transfers between devices  605 us (57%)
  blocking collectives  223 us (21%)
  other arithmetic  129 us (12%)
  matrix products  34.7 us (3%)
  local copies, waits for them, and re-layouts  34.1 us (3%)
  starting transfers between devices  19.7 us (2%)
  between operations  17.8 us (2%)
    psum x1, waiting for transfers between devices, local(): lax.psum(jnp.dot(sketch_rows.T, sketch_rows, precision=precise), ('tm', '...  268 us
    unnamed x5, waiting for transfers between devices  196 us
    psum x1, blocking collectives, local(): lax.psum((jnp.dot(error, hidden.T, precision=precise), jnp.sum(squared, a...  129 us
    another operation x14, other arithmetic, orthonormal(): lower = jnp.linalg.cholesky(gram)  82.2 us
    ppermute x7, waiting for transfers between devices, carry_outputs(): ready = lax.ppermute(ready, axis_name=axis_tag, perm=table)  59.3 us
    psum x1, waiting for transfers between devices, local(): lax.psum((jnp.dot(error, hidden.T, precision=precise), jnp.sum(squared, a...  45.1 us
    all_gather x1, blocking collectives, local(): lax.all_gather(loading_rows, 'tm', axis=0, tiled=True)  43.1 us
    another operation x3, other arithmetic, orthonormal(): return jax.scipy.linalg.solve_triangular(lower, sketch.T, lower=True).T  42.5 us
  transfers between devices with their start and end apart: 13, of which 11 were waited for; matrix products, arithmetic and copies ran while one was open for 2% of the time, Pallas kernels for 0%

profile of v1, /device:TPU:8, one launch (start us, length us, event | category | flops | bytes accessed | tf_op | source)
XLA Modules:
  0.0 1063.5 jit_solution(10137348709128261745)
XLA Ops:
  7.2 3.6 collective-permute-start
  10.9 8.8 collective-permute-done
  20.4 1.9 collective-permute-start.1
  22.3 7.5 collective-permute-done.1
  30.5 1.9 collective-permute-start.2
  32.4 9.1 collective-permute-done.2
  41.5 1.9 collective-permute-start.3
  43.9 10.2 collective-permute-done.3
  54.1 1.9 collective-permute-start.4
  56.1 10.0 collective-permute-done.4
  66.1 1.9 collective-permute-start.5
  68.0 1.0 constant_dynamic-update-slice_fusion.5
  69.0 1.0 constant_dynamic-update-slice_fusion.4
  70.0 6.5 collective-permute-done.5
  76.4 1.9 collective-permute-start.6
  78.4 7.2 collective-permute-done.6
  85.7 3.1 convolution_bitcast_fusion
  88.8 1.3 dynamic-slice.3
  90.9 196.0 %all-reduce.15.cloned.1.call-done = f32[768,512]{0,1:T(8,128)} async-done(((f32[768,512]{0,1:T(8,128)}), f32[768,512]{0,1:T(8,128)}) %all-reduce.15.cloned.1.call-update) | async-done | bytes 1572880
  286.9 1.2 constant_dynamic-slice_fusion.1
  288.1 2.0 fusion.66
  291.4 2.2 fusion.23
  294.3 268.2 %all-reduce.9.cloned.1.call-done = f32[512,512]{0,1:T(8,128)} async-done(((f32[512,512]{0,1:T(8,128)}), f32[512,512]{0,1:T(8,128)}) %all-reduce.9.cloned.1.call-update) | async-done | bytes 1048592 | tf_op jit(solution)/shard_map/psum | solution.py:88
  562.5 2.6 copy.25
  565.1 1.8 fusion.3
  566.9 1.0 copy-done.3
  567.9 11.7 %cholesky.104 = f32[128,128]{1,0:T(8,128)S(1)} custom-call(f32[128,128]{1,0:T(8,128)S(1)} %cholesky.266), custom_call_target="Cholesky" | custom-call | tf_op jit(solution)/shard_map/jit(cholesky)/cholesky | solution.py:37
  579.6 9.8 custom-call.31
  589.5 1.2 cholesky.224
  590.6 2.0 constant_dynamic-update-slice_fusion
  592.6 1.3 convolution_subtract_fusion
  594.5 12.5 %cholesky.217 = f32[128,128]{1,0:T(8,128)S(1)} custom-call(f32[128,128]{1,0:T(8,128)} %cholesky.270), custom_call_target="Cholesky" | custom-call | tf_op jit(solution)/shard_map/jit(cholesky)/cholesky | solution.py:37
  607.7 10.8 %custom-call.32 = f32[1,128,128]{1,2,0:T(8,128)S(1)} custom-call(f32[1,128,128]{2,1,0:T(8,128)} %get-tuple-element.31), custom_call_target="InvertDiagBlocksLowerTriangular" | custom-call | tf_op jit(solution)/shard_map/jit(cholesky)/cholesky | solution.py:37
  619.4 1.4 convolution_subtract_fusion.1
  620.9 11.7 %cholesky.238 = f32[128,128]{1,0:T(8,128)S(1)} custom-call(f32[128,128]{1,0:T(8,128)S(1)} %cholesky.275), custom_call_target="Cholesky" | custom-call | tf_op jit(solution)/shard_map/jit(cholesky)/cholesky | solution.py:37
  633.9 9.8 custom-call.33
  644.5 1.4 convolution_subtract_fusion.2
  645.9 11.9 %cholesky.255 = f32[128,128]{1,0:T(8,128)S(1)} custom-call(f32[128,128]{1,0:T(8,128)S(1)} %convolution_subtract_fusion.2), custom_call_target="Cholesky" | custom-call | tf_op jit(solution)/shard_map/jit(cholesky)/cholesky | solution.py:37
  662.3 2.4 select_select_fusion
  664.6 14.5 %while.1 = (s32[]{:T(128)}, f32[512,512]{1,0:T(8,128)}, s32[4,2]{0,1:T(2,128)S(1)}, f32[4,128,128]{2,1,0:T(8,128)}, s32[]{:T(128)}) while((s32[]{:T(128)}, f32[512,512]{1,0:T(8,128)}, s32[4,2]{0,1:T(2,128)S(1)}, f32[4,128,128]{2,1,0:T(8,128)}, s32[]{:T(128)}) %tuple.34), condition=%wide.while_cond, body=%wide.while_body.sunk | while | flops 2 | bytes 132205 | solution.py:38
  665.3 3.0 bitcast_dynamic-update-slice_fusion.2
  669.0 3.0 bitcast_dynamic-update-slice_fusion.2
  672.6 3.0 bitcast_dynamic-update-slice_fusion.2
  676.2 2.9 bitcast_dynamic-update-slice_fusion.2
  679.1 40.1 %custom-call.34 = f32[4,128,128]{1,2,0:T(8,128)S(1)} custom-call(f32[4,128,128]{2,1,0:T(8,128)} %get-tuple-element.10), custom_call_target="InvertDiagBlocksLowerTriangular" | custom-call | tf_op jit(solution)/shard_map/jit(_solve_triangular)/triangular_solve | solution.py:38
  720.1 1.0 convolution_subtract_fusion.5
  721.3 1.1 convolution_subtract_fusion.4
  722.7 1.3 convolution_subtract_fusion.3
  724.3 43.1 %all-gather = bf16[64,12,64]{2,1,0:T(8,128)(2,1)S(1)} all-gather(bf16[1,12,64]{2,1,0:T(8,128)(2,1)S(1)} %fusion.2), channel_id=1, replica_groups=mesh['tm'=64,'region'=8] {'tm'}, dimensions={0}, use_global_device_ids=true | all-gather | bytes 99840 | tf_op jit(solution)/shard_map/all_gather | solution.py:93
  768.2 2.4 fusion.67
  770.7 35.5 %all-reduce.16 = bf16[64,2048]{1,0:T(8,128)(2,1)S(1)} all-reduce(f32[64,2048]{1,0:T(8,128)} %fusion.23), channel_id=1, replica_groups=mesh['tm'=64,'region'=8] {'region'}, use_global_device_ids=true, to_apply=%region_11.12 | all-reduce | flops 131072 | bytes 786432 | tf_op jit(solution)/shard_map/psum | solution.py:101
  806.9 1.9 collective-permute-start.8
  808.8 36.6 %all-reduce.11.cloned.1.call-done = f32[64,2048]{1,0:T(8,128)} async-done(((f32[64,2048]{1,0:T(8,128)}), f32[64,2048]{1,0:T(8,128)}) %all-reduce.11.cloned.1.call-update) | async-done | bytes 524304 | tf_op jit(solution)/shard_map/psum | solution.py:101
  845.4 1.4 slice.142
  846.8 2.1 collective-permute-start.7
  849.8 2.8 copy.27
  852.6 1.9 multiply_reduce_fusion.2
  854.6 2.1 fusion.11
  856.7 2.5 multiply_reduce_fusion
  859.2 4.8 fusion.68
  864.0 129.4 %all-reduce.2 = (f32[64]{0:T(128)S(1)}, f32[768]{0:T(1024)S(1)}) all-reduce(f32[64]{0:T(128)S(1)} %get-tuple-element.38, f32[768]{0:T(1024)S(1)} %get-tuple-element.11), channel_id=1, replica_groups=mesh['tm'=64,'region'=8] {'tm'}, use_global_device_ids=true, to_apply=%region_18.19 | all-reduce | flops 832 | bytes 6656 | tf_op jit(solution)/shard_map/psum | solution.py:112
  993.5 15.0 %psum.52 = f32[2048]{0:T(1024)S(1)} all-reduce(f32[2048]{0:T(1024)S(1)} %get-tuple-element.12), channel_id=1, replica_groups=mesh['tm'=64,'region'=8] {'region'}, use_global_device_ids=true, to_apply=%region_13.14 | all-reduce | flops 2048 | bytes 16384 | tf_op jit(solution)/shard_map/psum | solution.py:120
  1009.0 45.1 %all-reduce.13.cloned.1.call-done = f32[768,64]{0,1:T(8,128)} async-done(((f32[768,64]{0,1:T(8,128)}), f32[768,64]{0,1:T(8,128)}) %all-reduce.13.cloned.1.call-update) | async-done | bytes 196624 | tf_op jit(solution)/shard_map/psum | solution.py:112
  1054.2 1.7 rsqrt_multiply_fusion
  (89 shorter events, 18.5 us)
Async XLA Ops:
  7.2 716.9 %copy-start = (f32[512,64]{0,1:T(8,128)S(1)}, f32[512,64]{0,1:T(8,128)}, u32[]{:S(2)}) copy-start(f32[512,64]{0,1:T(8,128)} %param.12) | copy-start | bytes 393220
  7.2 36.7 %copy-start.5 = (bf16[2048,64]{0,1:T(8,128)(2,1)S(1)}, bf16[2048,64]{0,1:T(8,128)(2,1)}, u32[]{:S(2)}) copy-start(bf16[2048,64]{0,1:T(8,128)(2,1)} %param.11) | copy-start | bytes 786436
  7.2 279.7 %all-reduce.15.cloned.1.call-start = ((), (), s32[]{:S(2)}) async-start(), calls=%async_computation.3 | async-start | bytes 3145728
  7.2 12.4 %collective-permute-start = (bf16[2048,64]{0,1:T(8,128)(2,1)}, bf16[2048,64]{0,1:T(8,128)(2,1)S(1)}, u32[]{:S(2)}, u32[]{:S(2)}) collective-permute-start(bf16[2048,64]{0,1:T(8,128)(2,1)} %param.11), channel_id=1, source_target_pairs={{0,1},{1,2},{2,3},{3,4},{4,5},{5,6},{6,7},{7,0},{8,9},{9,10},{10,1... | collective-permute-start | bytes 786440 | tf_op jit(solution)/shard_map/ppermute | solution.py:23
  19.7 0.7 copy-start.6
  20.4 9.5 collective-permute-start.1
  29.8 0.7 copy-start.8
  30.5 11.0 %collective-permute-start.2 = (bf16[2048,64]{0,1:T(8,128)(2,1)S(1)}, bf16[2048,64]{0,1:T(8,128)(2,1)}, u32[]{:S(2)}, u32[]{:S(2)}) collective-permute-start(bf16[2048,64]{0,1:T(8,128)(2,1)S(1)} %collective-permute-done.1), channel_id=1, source_target_pairs={{0,1},{1,2},{2,3},{3,4},{4,5},{5,6},{6,7},{7,0},{8,9},{9,10},{10,1... | collective-permute-start | bytes 786440 | tf_op jit(solution)/shard_map/ppermute | solution.py:23
  41.5 12.6 %collective-permute-start.3 = (bf16[2048,64]{0,1:T(8,128)(2,1)}, bf16[2048,64]{0,1:T(8,128)(2,1)}, u32[]{:S(2)}, u32[]{:S(2)}) collective-permute-start(bf16[2048,64]{0,1:T(8,128)(2,1)} %collective-permute-done.2), channel_id=1, source_target_pairs={{0,1},{1,2},{2,3},{3,4},{4,5},{5,6},{6,7},{7,0},{8,9},{9,10},{10,1... | collective-permute-start | bytes 786440 | tf_op jit(solution)/shard_map/ppermute | solution.py:23
  43.6 12.4 %copy-start.7 = (bf16[2048,64]{0,1:T(8,128)(2,1)S(1)}, bf16[2048,64]{0,1:T(8,128)(2,1)}, u32[]{:S(2)}) copy-start(bf16[2048,64]{0,1:T(8,128)(2,1)} %copy-done.6) | copy-start | bytes 786436
  43.6 12.5 %copy-start.9 = (bf16[2048,64]{0,1:T(8,128)(2,1)S(1)}, bf16[2048,64]{0,1:T(8,128)(2,1)}, u32[]{:S(2)}) copy-start(bf16[2048,64]{0,1:T(8,128)(2,1)} %copy-done.8) | copy-start | bytes 786436
  43.9 41.8 %copy-start.1 = (bf16[768,2048]{1,0:T(8,128)(2,1)S(1)}, bf16[768,2048]{1,0:T(8,128)(2,1)}, u32[]{:S(2)}) copy-start(bf16[768,2048]{1,0:T(8,128)(2,1)} %param.10) | copy-start | bytes 9437188
  54.1 12.0 %collective-permute-start.4 = (bf16[2048,64]{0,1:T(8,128)(2,1)}, bf16[2048,64]{0,1:T(8,128)(2,1)S(1)}, u32[]{:S(2)}, u32[]{:S(2)}) collective-permute-start(bf16[2048,64]{0,1:T(8,128)(2,1)} %collective-permute-done.3), channel_id=1, source_target_pairs={{0,1},{1,2},{2,3},{3,4},{4,5},{5,6},{6,7},{7,0},{8,9},{9,10},{10,1... | collective-permute-start | bytes 786440 | tf_op jit(solution)/shard_map/ppermute | solution.py:23
  66.1 10.3 collective-permute-start.5
  76.4 9.2 collective-permute-start.6
  85.7 5.1 copy-start.15
  88.7 202.6 %copy-start.11 = (bf16[768,8]{0,1:T(8,128)(2,1)S(1)}, bf16[768,8]{0,1:T(8,128)(2,1)}, u32[]{:S(2)}) copy-start(bf16[768,8]{0,1:T(8,128)(2,1)} %param.16) | copy-start | bytes 36868
  88.8 473.8 %all-reduce.9.cloned.1.call-start = ((), (), s32[]{:S(2)}) async-start(), calls=%async_computation | async-start | bytes 2097152 | tf_op jit(solution)/shard_map/psum | solution.py:88
  290.2 555.2 %all-reduce.11.cloned.1.call-start = ((), (), s32[]{:S(2)}) async-start(), calls=%async_computation.1 | async-start | bytes 1048576 | tf_op jit(solution)/shard_map/psum | solution.py:101
  566.9 1.0 copy-start.3
  768.2 80.7 %copy-start.14 = (s32[8,8]{1,0:T(8,128)S(1)}, s32[8,8]{1,0:T(8,128)}, u32[]{:S(2)}) copy-start(s32[8,8]{1,0:T(8,128)} %param.19) | copy-start | bytes 772
  770.6 283.5 %all-reduce.13.cloned.1.call-start = ((), (), s32[]{:S(2)}) async-start(), calls=%async_computation.2 | async-start | bytes 393216 | tf_op jit(solution)/shard_map/psum | solution.py:112
  806.9 49.8 %collective-permute-start.8 = (bf16[64,1]{1,0:T(8,128)(2,1)}, bf16[64,1]{1,0:T(8,128)(2,1)}, u32[]{:S(2)}, u32[]{:S(2)}) collective-permute-start(bf16[64,1]{1,0:T(8,128)(2,1)} %slice.144), channel_id=1, source_target_pairs={{0,8},{8,16},{16,24},{24,32},{32,40},{40,48},{48,56},{56,64},{64,7... | collective-permute-start | bytes 392 | tf_op jit(solution)/shard_map/ppermute | solution.py:33
  846.8 5.8 collective-permute-start.7
  849.8 2.8 copy-start.12
  849.8 2.8 copy-start.13
  854.6 2.1 copy-start.2
  854.6 2.1 copy-start.10
  859.2 196.7 %copy-start.4 = (f32[64,2048]{1,0:T(8,128)S(1)}, f32[64,2048]{1,0:T(8,128)}, u32[]{:S(2)}) copy-start(f32[64,2048]{1,0:T(8,128)} %all-reduce.11.cloned.1.call-done) | copy-start | bytes 1572868
Sparse Core Ops, SparseCore 0:
  88.9 197.9 all-reduce.14
  292.0 270.4 all-reduce.8
  770.8 74.5 all-reduce.10
  864.2 189.9 all-reduce.12
